TPU v7x, 32 devices: a whole 2x2x4 slice. The times are simulated.
32 devices in a mesh: group: 2 (over y), dp: 8 (over z, x), tensor: 2 (over core).
Axes of the slice: x: 2, y: 2, z: 4, core: 2. Of those that a mesh axis runs over, the one named last changes fastest.
Arguments:
- roll_inputs: bfloat16 [64, 128, 14336], P(('group', 'dp'), None, 'tensor'), parts along dimension 0, may hold values from -6 to 6
- roll_grads: bfloat16 [64, 128, 8192], P(('group', 'dp'), None, 'tensor'), parts along dimension 0, may hold values from -6 to 6
- ref_inputs: bfloat16 [16, 128, 14336], P(('group', 'dp'), None, 'tensor'), parts along dimension 0, may hold values from -6 to 6
- ref_grads: bfloat16 [16, 128, 8192], P(('group', 'dp'), None, 'tensor'), parts along dimension 0, may hold values from -6 to 6
- in_basis: bfloat16 [14336, 64], P('tensor'), may hold values from -0.046875 to 0.046875
- out_basis: bfloat16 [8192, 64], P('tensor'), may hold values from -0.0625 to 0.0625
- roll_lengths: int32 [64], P(('group', 'dp')), parts along dimension 0, may hold values from 1 to 128, 2112 in all
- ref_lengths: int32 [16], P(('group', 'dp')), parts along dimension 0, may hold values from 1 to 128, 576 in all
Outputs:
- scores: float32 [64, 8], P(('group', 'dp')), parts along dimension 0
There are 2 independent parts, one for each index of `group`. A program takes and returns all parts, laid end to end along the dimension named above; an argument that names none is the same for every part. Nothing has to cross between parts.
Inputs may be any that keep to these rules, and one draw needn't show every extreme that they name: `roll_lengths`: positions at or beyond a rollout's length are padding; some rollout has exactly 128 tokens. `ref_lengths`: positions at or beyond a reference prompt's length are padding; some reference prompt has exactly 128 tokens.
All inputs are finite; a program needn't handle non-finite values. No bound on the sum of `roll_lengths` or of `ref_lengths` on one device may be relied on, other than what follows from the above.
Results may differ from a plain program's by a relative error of at most 0.0003.
Values sent between devices are 32-bit elements; how exact they have to be, the bound alone decides.
No kernel may reach another device: no remote copies, remote signals or barrier semaphores. Data moves between devices by JAX's collectives and lax.ppermute only.
A program may use at most 64 MiB of HBM per device.

v0:
```python
import functools
import math

import jax
import jax.numpy as jnp
from jax import lax
from jax.experimental import pallas as pl
from jax.experimental.pallas import tpu as pltpu
from jax.sharding import PartitionSpec as P

STEP = 16
TILE = 32
REF_ROOM = 8 << 20
ROLL_ROOM = 8 << 20
EXACT = lax.Precision.HIGHEST


def columns(width):
    step = 1024 if width % 1024 == 0 else width
    return [(at, step) for at in range(0, width, step)]


def times_basis(rows, basis):
    return lax.dot_general(
        rows, basis, (((1,), (1,)), ((), ())), preferred_element_type=jnp.float32
    )


def ref_kernel(x_hbm, g_hbm, bx_hbm, bg_hbm, z_ref, bg, x, g, bx, sems):
    work = []
    for part, (src, basis_src, dst, basis_dst) in enumerate(
        ((x_hbm, bx_hbm, x, bx), (g_hbm, bg_hbm, g, bg))
    ):
        for at, step in columns(src.shape[2]):
            cut = pl.ds(at, step)
            k = len(work)
            copies = (
                pltpu.make_async_copy(basis_src.at[:, cut], basis_dst.at[:, cut], sems.at[0, k]),
                pltpu.make_async_copy(src.at[0, :, cut], dst.at[:, cut], sems.at[1, k]),
            )
            for copy in copies:
                copy.start()
            work.append((part, dst, basis_dst, cut, copies))
    sums = [None, None]
    for part, rows, basis, cut, copies in work:
        for copy in copies:
            copy.wait()
        term = times_basis(rows[:, cut], basis[:, cut])
        sums[part] = term if sums[part] is None else sums[part] + term
    z_ref[...] = jnp.concatenate([sums[1], sums[0]], axis=1)


def project_ref(x, g, bx, bg):
    span, wide_x, wide_g = x.shape[1], x.shape[2], g.shape[2]
    parts = len(columns(wide_x)) + len(columns(wide_g))
    return pl.pallas_call(
        ref_kernel,
        out_shape=(
            jax.ShapeDtypeStruct((span, bx.shape[0] + bg.shape[0]), jnp.float32),
            jax.ShapeDtypeStruct(bg.shape, bg.dtype),
        ),
        in_specs=[pl.BlockSpec(memory_space=pl.ANY)] * 4,
        out_specs=(pl.BlockSpec(memory_space=pltpu.VMEM),) * 2,
        scratch_shapes=[
            pltpu.VMEM((span, wide_x), x.dtype),
            pltpu.VMEM((span, wide_g), g.dtype),
            pltpu.VMEM(bx.shape, bx.dtype),
            pltpu.SemaphoreType.DMA((2, parts)),
        ],
        compiler_params=pltpu.CompilerParams(vmem_limit_bytes=REF_ROOM),
        cost_estimate=pl.CostEstimate(flops=20_000_000_000, bytes_accessed=60 << 20, transcendentals=0),
    )(*(pltpu.with_memory_space_constraint(a, pltpu.HBM) for a in (x, g, bx, bg)))


def sketch_of(z):
    half = z.shape[1] // 2
    full = lax.dot_general(
        z[:, :half], z[:, half:], (((0,), (0,)), ((), ())),
        preferred_element_type=jnp.float32, precision=EXACT,
    )
    rows = half // 2
    return jnp.concatenate([full[:rows], full[rows:]], axis=1)


def sketch_kernel(len_ref, own_ref, other_ref, sketch_ref):
    z = own_ref[...] + other_ref[...]
    keep = lax.broadcasted_iota(jnp.int32, z.shape, 0) < len_ref[...]
    sketch_ref[...] = sketch_of(jnp.where(keep, z, 0.0))


def ref_sketch(length, own, other):
    half = own.shape[1] // 2
    return pl.pallas_call(
        sketch_kernel,
        out_shape=jax.ShapeDtypeStruct((half // 2, half * 2), jnp.float32),
        in_specs=[pl.BlockSpec(memory_space=pltpu.VMEM)] * 3,
        out_specs=pl.BlockSpec(memory_space=pltpu.VMEM),
        compiler_params=pltpu.CompilerParams(vmem_limit_bytes=8 << 20),
    )(length, own, other)


def by_length(lens, rolls):
    ranks = []
    for i in range(rolls):
        rank = jnp.int32(0)
        for j in range(rolls):
            if j != i:
                ahead = lens[j] >= lens[i] if j < i else lens[j] > lens[i]
                rank = rank + ahead.astype(jnp.int32)
        ranks.append(rank)
    return [
        sum(jnp.where(ranks[i] == place, jnp.int32(i), 0) for i in range(rolls))
        for place in range(rolls)
    ], ranks


def steps_of(length):
    return (length + (STEP - 1)) // STEP


def roll_kernel(places, after_ref, lens, x_ref, g_ref, bx_ref, bg_ref, z_ref):
    rolls, span, _ = x_ref.shape
    numbers, _ = by_length(lens, rolls)
    half = bg_ref.shape[0]

    @pl.loop(0, len(places))
    def _(slot):
        roll = sum(jnp.where(slot == k, numbers[p], 0) for k, p in enumerate(places))
        need = (lens[roll] + (TILE - 1)) // TILE
        for tiles in range(1, span // TILE + 1):

            @pl.when(need == tiles)
            def _():
                rows = pl.ds(0, tiles * TILE)
                for k, (src, basis) in enumerate(((g_ref, bg_ref), (x_ref, bx_ref))):
                    z_ref[slot, rows, k * half : (k + 1) * half] = times_basis(
                        src[roll, rows, :], basis[...]
                    )


def project_rolls(places, after, x, g, bx, bg, lengths):
    rolls, span, wide_x = x.shape
    wide_g = g.shape[2]
    count = len(places)
    held = pl.BlockSpec(memory_space=pltpu.VMEM)
    return pl.pallas_call(
        functools.partial(roll_kernel, places),
        out_shape=jax.ShapeDtypeStruct((count, span, bx.shape[0] * 2), jnp.float32),
        in_specs=[
            pl.BlockSpec(memory_space=pl.ANY),
            pl.BlockSpec(memory_space=pltpu.SMEM),
            held, held, held, held,
        ],
        out_specs=held,
        compiler_params=pltpu.CompilerParams(vmem_limit_bytes=ROLL_ROOM),
        cost_estimate=pl.CostEstimate(
            flops=2 * count * span * (wide_x + wide_g) * 64,
            bytes_accessed=6 << 20,
            transcendentals=0,
        ),
    )(after, lengths, x, g, bx, bg)


def units_kernel(shares, lens, *refs):
    unit_ref = refs[-1]
    rolls = lens.shape[0]
    _, ranks = by_length(lens, rolls)
    span = refs[0].shape[1]
    for share, places in enumerate(shares):
        own_ref, other_ref = refs[2 * share : 2 * share + 2]
        for slot, place in enumerate(places):
            roll = sum(jnp.where(ranks[i] == place, jnp.int32(i), 0) for i in range(rolls))
            z = own_ref[slot] + other_ref[slot]
            keep = lax.broadcasted_iota(jnp.int32, z.shape, 0) < lens[roll]
            sketch = sketch_of(jnp.where(keep, z, 0.0))
            square = jnp.sum(sketch * sketch, axis=(0, 1), keepdims=True)
            size = sketch.shape[0] * sketch.shape[1]
            unit_ref[roll] = sketch / (jnp.sqrt(square / size + 1e-6) * math.sqrt(size))


def roll_units(shares, lengths, parts):
    rolls = lengths.shape[0]
    half = parts[0][0].shape[2] // 2
    flat = [z for pair in parts for z in pair]
    return pl.pallas_call(
        functools.partial(units_kernel, shares),
        out_shape=jax.ShapeDtypeStruct((rolls, half // 2, half * 2), jnp.float32),
        in_specs=[pl.BlockSpec(memory_space=pltpu.SMEM)]
        + [pl.BlockSpec(memory_space=pltpu.VMEM)] * len(flat),
        out_specs=pl.BlockSpec(memory_space=pltpu.VMEM),
        compiler_params=pltpu.CompilerParams(vmem_limit_bytes=8 << 20),
    )(lengths, *flat)


def score_kernel(order, dp_axis, unit_ref, *refs):
    sketch_refs, out_ref = refs[:-1], refs[-1]
    rolls = unit_ref.shape[0]
    total = len(order)
    me = lax.axis_index(dp_axis)
    lanes = unit_ref.shape[2]
    place = lax.broadcasted_iota(jnp.int32, (total, lanes), 0)
    tables = [jnp.zeros((total, lanes), jnp.float32) for _ in range(rolls + 1)]
    size = unit_ref.shape[1] * lanes
    at = 0
    for ref in sketch_refs:
        for i in range(ref.shape[0]):
            sketch = ref[i]
            here = place == jnp.bitwise_xor(me, order[at])
            for k in range(rolls + 1):
                other = unit_ref[k] if k < rolls else sketch
                row = jnp.sum(sketch * other, axis=0, keepdims=True)
                tables[k] = jnp.where(here, row, tables[k])
            at += 1
    ones = jnp.ones((8, lanes), jnp.float32)
    added = [
        lax.dot_general(
            ones, table, (((1,), (1,)), ((), ())),
            preferred_element_type=jnp.float32, precision=EXACT,
        )
        for table in tables
    ]
    spread = jnp.sqrt(added[rolls] / size + 1e-6)
    out_ref[...] = jnp.concatenate([(added[k] / spread)[0:1] for k in range(rolls)], axis=0)


def score(units, sketches, order):
    return pl.pallas_call(
        functools.partial(score_kernel, order, "dp"),
        out_shape=jax.ShapeDtypeStruct((units.shape[0], len(order)), jnp.float32),
        in_specs=[pl.BlockSpec(memory_space=pltpu.VMEM)] * (1 + len(sketches)),
        out_specs=pl.BlockSpec(memory_space=pltpu.VMEM),
        compiler_params=pltpu.CompilerParams(vmem_limit_bytes=8 << 20),
    )(units, *sketches)


def other_core(value):
    return lax.ppermute(value, "tensor", [(0, 1), (1, 0)])


def on_device(
    devices, roll_inputs, roll_grads, ref_inputs, ref_grads, in_basis, out_basis,
    roll_lengths, ref_lengths,
):
    bx, bg = in_basis.T, out_basis.T
    shares = ((0, 3), (1, 2))
    ref_z, bg = project_ref(ref_inputs, ref_grads, bx, bg)
    sketch = ref_sketch(ref_lengths[None], ref_z, other_core(ref_z))

    held = sketch[None]
    order = [0]
    bits = [1 << k for k in range(devices.bit_length() - 1)][::-1]
    parts = []
    for step, bit in enumerate(bits):
        got = lax.ppermute(held, "dp", [(i, i ^ bit) for i in range(devices)])
        if step < len(shares):
            z = project_rolls(shares[step], held, roll_inputs, roll_grads, bx, bg, roll_lengths)
            got, z = lax.optimization_barrier((got, z))
            parts.append((z, other_core(z)))
        order = order + [k ^ bit for k in order]
        if step < len(bits) - 1:
            held = jnp.concatenate([held, got], axis=0)
    units = roll_units(shares, roll_lengths, parts)
    return score(units, (held, got), tuple(order))


def solution(mesh):
    placed = (
        P(("group", "dp"), None, "tensor"),
        P(("group", "dp"), None, "tensor"),
        P(("group", "dp"), None, "tensor"),
        P(("group", "dp"), None, "tensor"),
        P("tensor", None),
        P("tensor", None),
        P(("group", "dp")),
        P(("group", "dp")),
    )
    return jax.shard_map(
        functools.partial(on_device, mesh.shape["dp"]),
        mesh=mesh,
        in_specs=placed,
        out_specs=P(("group", "dp"), None),
        check_vma=False,
    )
```

profile of v0, /device:TPU:0, one launch (start us, length us, event | category | flops | bytes accessed | tf_op | source)
XLA Modules:
  0.0 21.3 jit_solution(17645232037251830687)
XLA Ops:
  0.0 0.0 slice-start
  0.0 0.0 slice-start.1
  0.0 0.0 copy-start
  0.0 0.0 copy-start.1
  0.0 0.0 copy-start.2
  0.0 3.5 %shard_map.82 = (f32[128,128]{1,0:T(8,128)S(1)}, bf16[64,4096]{1,0:T(8,128)(2,1)S(1)}) custom-call(bf16[1,128,7168]{2,1,0:T(8,128)(2,1)} %x_hbm.1, bf16[1,128,4096]{2,1,0:T(8,128)(2,1)} %g_hbm.1, bf16[64,7168]{1,0:T(8,128)(2,1)} %bitcast.7, bf16[64,4096]{1,0:T(8,128)(2,1)} %bitcast.14), custom_call_target="tpu_custom_call" | custom-call | flops 20000000000 | bytes 62914560 | tf_op jit(solution)/shard_map/pallas_call | solution.py:56
  3.5 0.5 %collective-permute-start = (f32[128,128]{1,0:T(8,128)S(1)}, f32[128,128]{1,0:T(8,128)S(1)}, u32[]{:S(2)}, u32[]{:S(2)}) collective-permute-start(f32[128,128]{1,0:T(8,128)S(1)} %get-tuple-element.11.own_ref), channel_id=1, source_target_pairs={{0,1},{1,0},{2,3},{3,2},{4,5},{5,4},{6,7},{7,6},{8,9},{9,8},{10,11... | collective-permute-start | bytes 196616 | tf_op jit(solution)/shard_map/ppermute | solution.py:237
  5.5 0.0 collective-permute-done.other_ref
  5.5 0.4 %shard_map.83 = f32[32,128]{1,0:T(8,128)S(1)} custom-call(s32[1,1]{1,0:T(1,128)} %bitcast.4.len_ref, f32[128,128]{1,0:T(8,128)S(1)} %get-tuple-element.11.own_ref, f32[128,128]{1,0:T(8,128)S(1)} %collective-permute-done.other_ref), custom_call_target="tpu_custom_call" | custom-call | tf_op jit(solution)/shard_map/pallas_call | solution.py:93
  5.9 3.6 %collective-permute-start.1 = (f32[1,32,128]{2,1,0:T(8,128)S(1)}, f32[1,32,128]{2,1,0:T(8,128)S(1)}, u32[]{:S(2)}, u32[]{:S(2)}) collective-permute-start(f32[1,32,128]{2,1,0:T(8,128)S(1)} %bitcast.10), channel_id=1, source_target_pairs={{0,8},{2,10},{4,12},{6,14},{8,0},{10,2},{12,4},{14,6},{1,9},{3,11}... | collective-permute-start | bytes 49160 | tf_op jit(solution)/shard_map/ppermute | solution.py:254
  9.5 0.0 slice-done
  9.5 0.0 slice-done.1
  9.5 0.0 copy-done
  9.5 0.0 copy-done.1
  9.5 0.0 copy-done.2
  9.5 2.1 %shard_map.84.refs_0_ = f32[2,128,128]{2,1,0:T(8,128)S(1)} custom-call(f32[1,32,128]{2,1,0:T(8,128)S(1)} %bitcast.11, s32[4]{0:T(128)S(1)} %copy-done.2, bf16[4,128,7168]{2,1,0:T(8,128)(2,1)S(1)} %bitcast.6, bf16[4,128,4096]{2,1,0:T(8,128)(2,1)S(1)} %copy-done, bf16[64,7168]{1,0:T(8,128)(2,1)S(1)} %bitcast.8, bf16[64,4096]{1,0:T(8,128)(2,1)S(1)} %get-tuple-element.12.bg_ref), custom_call_target="tpu_custom_call" | custom-call | flops 369098752 | bytes 6291456 | tf_op jit(solution)/shard_map/pallas_call | solution.py:146
  11.6 0.0 collective-permute-done.1
  11.7 1.6 %collective-permute-start.3 = (f32[2,32,128]{2,1,0:T(8,128)S(1)}, f32[2,32,128]{2,1,0:T(8,128)S(1)}, u32[]{:S(2)}, u32[]{:S(2)}) collective-permute-start(f32[2,32,128]{2,1,0:T(8,128)S(1)} %pad_maximum_fusion.1.after_ref), channel_id=1, source_target_pairs={{0,4},{2,6},{4,0},{6,2},{8,12},{10,14},{12,8},{14,10},{1,5},{3,7},... | collective-permute-start | bytes 98312 | tf_op jit(solution)/shard_map/ppermute | solution.py:254
  13.3 0.0 collective-permute-start.2
  13.3 2.3 %shard_map.85.refs_2_ = f32[2,128,128]{2,1,0:T(8,128)S(1)} custom-call(f32[2,32,128]{2,1,0:T(8,128)S(1)} %pad_maximum_fusion.1.after_ref, s32[4]{0:T(128)S(1)} %copy-done.2, bf16[4,128,7168]{2,1,0:T(8,128)(2,1)S(1)} %bitcast.6, bf16[4,128,4096]{2,1,0:T(8,128)(2,1)S(1)} %copy-done, bf16[64,7168]{1,0:T(8,128)(2,1)S(1)} %bitcast.9, ...), custom_call_target="tpu_custom_call" | custom-call | flops 369098752 | bytes 6291456 | tf_op jit(solution)/shard_map/pallas_call | solution.py:146
  15.6 0.0 collective-permute-done.3
  15.7 0.6 %collective-permute-start.4 = (f32[2,128,128]{2,1,0:T(8,128)S(1)}, f32[2,128,128]{2,1,0:T(8,128)S(1)}, u32[]{:S(2)}, u32[]{:S(2)}) collective-permute-start(f32[2,128,128]{2,1,0:T(8,128)S(1)} %shard_map.85.refs_2_), channel_id=1, source_target_pairs={{0,1},{1,0},{2,3},{3,2},{4,5},{5,4},{6,7},{7,6},{8,9},{9,8},{10,11... | collective-permute-start | bytes 393224 | tf_op jit(solution)/shard_map/ppermute | solution.py:237
  16.2 0.8 %collective-permute-start.5 = (f32[4,32,128]{2,1,0:T(8,128)S(1)}, f32[4,32,128]{2,1,0:T(8,128)S(1)}, u32[]{:S(2)}, u32[]{:S(2)}) collective-permute-start(f32[4,32,128]{2,1,0:T(8,128)S(1)} %pad_maximum_fusion.refs_0_), channel_id=1, source_target_pairs={{0,2},{2,0},{4,6},{6,4},{8,10},{10,8},{12,14},{14,12},{1,3},{3,1},... | collective-permute-start | bytes 196616 | tf_op jit(solution)/shard_map/ppermute | solution.py:254
  17.0 0.0 collective-permute-done.2.refs_1_
  17.0 0.2 collective-permute-done.4.refs_3_
  17.2 1.2 %shard_map.86.unit_ref = f32[4,32,128]{2,1,0:T(8,128)S(1)} custom-call(s32[4]{0:T(128)S(1)} %copy-done.2, f32[2,128,128]{2,1,0:T(8,128)S(1)} %shard_map.84.refs_0_, f32[2,128,128]{2,1,0:T(8,128)S(1)} %collective-permute-done.2.refs_1_, f32[2,128,128]{2,1,0:T(8,128)S(1)} %shard_map.85.refs_2_, f32[2,128,128]{2,1,0:T(8,128)S(1)} %collective-permute-done.4.refs_3_), custom_call_target="tpu_custom_call" | custom-call | tf_op jit(solution)/shard_map/pallas_call | solution.py:185
  18.4 2.1 %collective-permute-done.5.refs_1_ = f32[4,32,128]{2,1,0:T(8,128)S(1)} collective-permute-done((f32[4,32,128]{2,1,0:T(8,128)S(1)}, f32[4,32,128]{2,1,0:T(8,128)S(1)}, u32[]{:S(2)}, u32[]{:S(2)}) %collective-permute-start.5) | collective-permute-done | bytes 65568 | tf_op jit(solution)/shard_map/ppermute | solution.py:254
  20.5 0.8 %shard_map.87 = f32[4,8]{1,0:T(4,128)} custom-call(f32[4,32,128]{2,1,0:T(8,128)S(1)} %shard_map.86.unit_ref, f32[4,32,128]{2,1,0:T(8,128)S(1)} %pad_maximum_fusion.refs_0_, f32[4,32,128]{2,1,0:T(8,128)S(1)} %collective-permute-done.5.refs_1_), custom_call_target="tpu_custom_call" | custom-call | tf_op jit(solution)/shard_map/pallas_call | solution.py:227
  (3 shorter events, 0.0 us)
Async XLA Ops:
  0.0 9.5 %slice-start = ((s8[7340032]{0:T(1024)(128)(4,1)}), s8[4194304]{0:T(1024)(128)(4,1)S(1)}, s32[]{:S(2)}) async-start(s8[7340032]{0:T(1024)(128)(4,1)} %bitcast.5), calls=%async_computation | async-start | bytes 8388608
  0.0 9.5 %slice-start.1 = ((s8[7340032]{0:T(1024)(128)(4,1)}), s8[3145728]{0:T(1024)(128)(4,1)S(1)}, s32[]{:S(2)}) async-start(s8[7340032]{0:T(1024)(128)(4,1)} %bitcast.5), calls=%async_computation.1 | async-start | bytes 6291456
  0.0 9.5 %copy-start = (bf16[4,128,4096]{2,1,0:T(8,128)(2,1)S(1)}, bf16[4,128,4096]{2,1,0:T(8,128)(2,1)}, u32[]{:S(2)}) copy-start(bf16[4,128,4096]{2,1,0:T(8,128)(2,1)} %g_ref.3) | copy-start | bytes 12582916
  0.0 9.5 %copy-start.1 = (bf16[7168,64]{0,1:T(8,128)(2,1)S(1)}, bf16[7168,64]{0,1:T(8,128)(2,1)}, u32[]{:S(2)}) copy-start(bf16[7168,64]{0,1:T(8,128)(2,1)} %param.12) | copy-start | bytes 2752516
  0.0 9.5 %copy-start.2 = (s32[4]{0:T(128)S(1)}, s32[4]{0:T(128)}, u32[]{:S(2)}) copy-start(s32[4]{0:T(128)} %lens.5) | copy-start | bytes 52
  3.5 2.0 %collective-permute-start = (f32[128,128]{1,0:T(8,128)S(1)}, f32[128,128]{1,0:T(8,128)S(1)}, u32[]{:S(2)}, u32[]{:S(2)}) collective-permute-start(f32[128,128]{1,0:T(8,128)S(1)} %get-tuple-element.11.own_ref), channel_id=1, source_target_pairs={{0,1},{1,0},{2,3},{3,2},{4,5},{5,4},{6,7},{7,6},{8,9},{9,8},{10,11... | collective-permute-start | bytes 196616 | tf_op jit(solution)/shard_map/ppermute | solution.py:237
  5.9 5.7 %collective-permute-start.1 = (f32[1,32,128]{2,1,0:T(8,128)S(1)}, f32[1,32,128]{2,1,0:T(8,128)S(1)}, u32[]{:S(2)}, u32[]{:S(2)}) collective-permute-start(f32[1,32,128]{2,1,0:T(8,128)S(1)} %bitcast.10), channel_id=1, source_target_pairs={{0,8},{2,10},{4,12},{6,14},{8,0},{10,2},{12,4},{14,6},{1,9},{3,11}... | collective-permute-start | bytes 49160 | tf_op jit(solution)/shard_map/ppermute | solution.py:254
  11.7 4.0 %collective-permute-start.3 = (f32[2,32,128]{2,1,0:T(8,128)S(1)}, f32[2,32,128]{2,1,0:T(8,128)S(1)}, u32[]{:S(2)}, u32[]{:S(2)}) collective-permute-start(f32[2,32,128]{2,1,0:T(8,128)S(1)} %pad_maximum_fusion.1.after_ref), channel_id=1, source_target_pairs={{0,4},{2,6},{4,0},{6,2},{8,12},{10,14},{12,8},{14,10},{1,5},{3,7},... | collective-permute-start | bytes 98312 | tf_op jit(solution)/shard_map/ppermute | solution.py:254
  13.3 3.7 %collective-permute-start.2 = (f32[2,128,128]{2,1,0:T(8,128)S(1)}, f32[2,128,128]{2,1,0:T(8,128)S(1)}, u32[]{:S(2)}, u32[]{:S(2)}) collective-permute-start(f32[2,128,128]{2,1,0:T(8,128)S(1)} %shard_map.84.refs_0_), channel_id=1, source_target_pairs={{0,1},{1,0},{2,3},{3,2},{4,5},{5,4},{6,7},{7,6},{8,9},{9,8},{10,11... | collective-permute-start | bytes 393224 | tf_op jit(solution)/shard_map/ppermute | solution.py:237
  15.7 1.6 %collective-permute-start.4 = (f32[2,128,128]{2,1,0:T(8,128)S(1)}, f32[2,128,128]{2,1,0:T(8,128)S(1)}, u32[]{:S(2)}, u32[]{:S(2)}) collective-permute-start(f32[2,128,128]{2,1,0:T(8,128)S(1)} %shard_map.85.refs_2_), channel_id=1, source_target_pairs={{0,1},{1,0},{2,3},{3,2},{4,5},{5,4},{6,7},{7,6},{8,9},{9,8},{10,11... | collective-permute-start | bytes 393224 | tf_op jit(solution)/shard_map/ppermute | solution.py:237
  16.2 4.3 %collective-permute-start.5 = (f32[4,32,128]{2,1,0:T(8,128)S(1)}, f32[4,32,128]{2,1,0:T(8,128)S(1)}, u32[]{:S(2)}, u32[]{:S(2)}) collective-permute-start(f32[4,32,128]{2,1,0:T(8,128)S(1)} %pad_maximum_fusion.refs_0_), channel_id=1, source_target_pairs={{0,2},{2,0},{4,6},{6,4},{8,10},{10,8},{12,14},{14,12},{1,3},{3,1},... | collective-permute-start | bytes 196616 | tf_op jit(solution)/shard_map/ppermute | solution.py:254
where the time goes:
time: 21.4 us; the launch traced here: 21.3 us
  Pallas kernels  10.4 us (49%)
  starting transfers between devices  7.14 us (33%)
  waiting for transfers between devices  2.26 us (11%)
  between operations  1.52 us (7%)
    ppermute x3, starting transfers between devices, on_device(): got = lax.ppermute(held, 'dp', [(i, i ^ bit) for i in range(devices)])  6.04 us
    pallas_call x2, Pallas kernels, project_rolls(): pl.pallas_call(functools.partial(roll_kernel, places), out_shape=jax.Shap...  4.44 us
    pallas_call x1, Pallas kernels, project_ref(): pl.pallas_call(ref_kernel, out_shape=(jax.ShapeDtypeStruct((span, bx.shap...  3.47 us
    ppermute x3, waiting for transfers between devices, on_device(): got = lax.ppermute(held, 'dp', [(i, i ^ bit) for i in range(devices)])  2.07 us
    pallas_call x1, Pallas kernels, roll_units(): pl.pallas_call(functools.partial(units_kernel, shares), out_shape=jax.Sha...  1.22 us
    ppermute x3, starting transfers between devices, other_core(): return lax.ppermute(value, 'tensor', [(0, 1), (1, 0)])  1.1 us
    pallas_call x1, Pallas kernels, score(): pl.pallas_call(functools.partial(score_kernel, order, 'dp'), out_shape=ja...  0.84 us
  transfers between devices with their start and end apart: 6, of which 2 were waited for; matrix products, arithmetic and copies ran while one was open for 0% of the time, Pallas kernels for 27%

commit v1 on v0

--- a/solution.py
+++ b/solution.py
@@ -8,7 +8,7 @@
 from jax.experimental.pallas import tpu as pltpu
 from jax.sharding import PartitionSpec as P
 
-STEP = 16
+CHUNK = 2048
 TILE = 32
 REF_ROOM = 8 << 20
 ROLL_ROOM = 8 << 20
@@ -16,8 +16,7 @@
 
 
 def columns(width):
-    step = 1024 if width % 1024 == 0 else width
-    return [(at, step) for at in range(0, width, step)]
+    return [(at, min(CHUNK, width - at)) for at in range(0, width, CHUNK)]
 
 
 def times_basis(rows, basis):
@@ -26,7 +25,7 @@
     )
 
 
-def ref_kernel(x_hbm, g_hbm, bx_hbm, bg_hbm, z_ref, bg, x, g, bx, sems):
+def ref_kernel(x_hbm, g_hbm, bx_hbm, bg_hbm, z_ref, bx, bg, x, g, sems):
     work = []
     for part, (src, basis_src, dst, basis_dst) in enumerate(
         ((x_hbm, bx_hbm, x, bx), (g_hbm, bg_hbm, g, bg))
@@ -57,14 +56,14 @@
         ref_kernel,
         out_shape=(
             jax.ShapeDtypeStruct((span, bx.shape[0] + bg.shape[0]), jnp.float32),
+            jax.ShapeDtypeStruct(bx.shape, bx.dtype),
             jax.ShapeDtypeStruct(bg.shape, bg.dtype),
         ),
         in_specs=[pl.BlockSpec(memory_space=pl.ANY)] * 4,
-        out_specs=(pl.BlockSpec(memory_space=pltpu.VMEM),) * 2,
+        out_specs=(pl.BlockSpec(memory_space=pltpu.VMEM),) * 3,
         scratch_shapes=[
             pltpu.VMEM((span, wide_x), x.dtype),
             pltpu.VMEM((span, wide_g), g.dtype),
-            pltpu.VMEM(bx.shape, bx.dtype),
             pltpu.SemaphoreType.DMA((2, parts)),
         ],
         compiler_params=pltpu.CompilerParams(vmem_limit_bytes=REF_ROOM),
@@ -84,7 +83,7 @@
 
 def sketch_kernel(len_ref, own_ref, other_ref, sketch_ref):
     z = own_ref[...] + other_ref[...]
-    keep = lax.broadcasted_iota(jnp.int32, z.shape, 0) < len_ref[...]
+    keep = lax.broadcasted_iota(jnp.int32, z.shape, 0) < len_ref[0]
     sketch_ref[...] = sketch_of(jnp.where(keep, z, 0.0))
 
 
@@ -93,7 +92,8 @@
     return pl.pallas_call(
         sketch_kernel,
         out_shape=jax.ShapeDtypeStruct((half // 2, half * 2), jnp.float32),
-        in_specs=[pl.BlockSpec(memory_space=pltpu.VMEM)] * 3,
+        in_specs=[pl.BlockSpec(memory_space=pltpu.SMEM)]
+        + [pl.BlockSpec(memory_space=pltpu.VMEM)] * 2,
         out_specs=pl.BlockSpec(memory_space=pltpu.VMEM),
         compiler_params=pltpu.CompilerParams(vmem_limit_bytes=8 << 20),
     )(length, own, other)
@@ -237,21 +237,30 @@
     return lax.ppermute(value, "tensor", [(0, 1), (1, 0)])
 
 
+def from_chip(value, bit, devices, cores):
+    pairs = [
+        (i * cores + t, (i ^ bit) * cores + (t + 1) % cores)
+        for i in range(devices)
+        for t in range(cores)
+    ]
+    return lax.ppermute(value, ("dp", "tensor"), pairs)
+
+
 def on_device(
-    devices, roll_inputs, roll_grads, ref_inputs, ref_grads, in_basis, out_basis,
+    devices, cores, roll_inputs, roll_grads, ref_inputs, ref_grads, in_basis, out_basis,
     roll_lengths, ref_lengths,
 ):
     bx, bg = in_basis.T, out_basis.T
     shares = ((0, 3), (1, 2))
-    ref_z, bg = project_ref(ref_inputs, ref_grads, bx, bg)
-    sketch = ref_sketch(ref_lengths[None], ref_z, other_core(ref_z))
+    ref_z, bx, bg = project_ref(ref_inputs, ref_grads, bx, bg)
+    sketch = ref_sketch(ref_lengths, ref_z, other_core(ref_z))
 
     held = sketch[None]
     order = [0]
     bits = [1 << k for k in range(devices.bit_length() - 1)][::-1]
     parts = []
     for step, bit in enumerate(bits):
-        got = lax.ppermute(held, "dp", [(i, i ^ bit) for i in range(devices)])
+        got = from_chip(held, bit, devices, cores)
         if step < len(shares):
             z = project_rolls(shares[step], held, roll_inputs, roll_grads, bx, bg, roll_lengths)
             got, z = lax.optimization_barrier((got, z))
@@ -275,7 +284,7 @@
         P(("group", "dp")),
     )
     return jax.shard_map(
-        functools.partial(on_device, mesh.shape["dp"]),
+        functools.partial(on_device, mesh.shape["dp"], mesh.shape["tensor"]),
         mesh=mesh,
         in_specs=placed,
         out_specs=P(("group", "dp"), None),

time: 21.4 us -> 20.1 us (0.939)
  Pallas kernels: 10.4 us -> 9.53 us
  waiting for transfers between devices: 2.26 us -> 1.55 us
  starting transfers between devices: 7.14 us -> 7.45 us
    pallas_call x2, Pallas kernels: 4.44 us -> 3.87 us  [project_rolls(): pl.pallas_call(functools.partial(roll_kernel, places), out_shape=jax.Shap...]
    ppermute x3, waiting for transfers between devices: 2.07 us -> 1.54 us  [from_chip(): return lax.ppermute(value, ('dp', 'tensor'), pairs)]
    ppermute x3, starting transfers between devices: 6.04 us -> 6.36 us  [from_chip(): return lax.ppermute(value, ('dp', 'tensor'), pairs)]
  transfers between devices with their start and end apart: 6 -> 6, of which waited for: 2 -> 1; matrix products, arithmetic and copies ran while one was open for 0% -> 0% of each run, Pallas kernels for 27% -> 25%
where the time goes in v1:
time: 20.1 us
  Pallas kernels  9.53 us (47%)
  starting transfers between devices  7.45 us (37%)
  waiting for transfers between devices  1.55 us (8%)
  between operations  1.5 us (7%)
    ppermute x3, starting transfers between devices, from_chip(): return lax.ppermute(value, ('dp', 'tensor'), pairs)  6.36 us
    pallas_call x2, Pallas kernels, project_rolls(): pl.pallas_call(functools.partial(roll_kernel, places), out_shape=jax.Shap...  3.87 us
    pallas_call x1, Pallas kernels, project_ref(): pl.pallas_call(ref_kernel, out_shape=(jax.ShapeDtypeStruct((span, bx.shap...  3.27 us
    ppermute x3, waiting for transfers between devices, from_chip(): return lax.ppermute(value, ('dp', 'tensor'), pairs)  1.54 us
    pallas_call x1, Pallas kernels, roll_units(): pl.pallas_call(functools.partial(units_kernel, shares), out_shape=jax.Sha...  1.22 us
    ppermute x3, starting transfers between devices, other_core(): return lax.ppermute(value, 'tensor', [(0, 1), (1, 0)])  1.09 us
    pallas_call x1, Pallas kernels, score(): pl.pallas_call(functools.partial(score_kernel, order, 'dp'), out_shape=ja...  0.84 us
  transfers between devices with their start and end apart: 6, of which 1 were waited for; matrix products, arithmetic and copies ran while one was open for 0% of the time, Pallas kernels for 25%

profile of v1, /device:TPU:0, one launch (start us, length us, event | category | flops | bytes accessed | tf_op | source)
XLA Modules:
  0.0 20.1 jit_solution(2948058573212437488)
XLA Ops:
  0.0 0.0 slice-start
  0.0 0.0 slice-start.1
  0.0 0.0 copy-start
  0.0 0.0 copy-start.1
  0.0 3.3 %shard_map.82 = (f32[128,128]{1,0:T(8,128)S(1)}, bf16[64,7168]{1,0:T(8,128)(2,1)S(1)}, bf16[64,4096]{1,0:T(8,128)(2,1)S(1)}) custom-call(bf16[1,128,7168]{2,1,0:T(8,128)(2,1)} %x_hbm.1, bf16[1,128,4096]{2,1,0:T(8,128)(2,1)} %g_hbm.1, bf16[64,7168]{1,0:T(8,128)(2,1)} %bitcast.9, bf16[64,4096]{1,0:T(8,128)(2,1)} %bitcast.10), custom_call_target="tpu_custom_call" | custom-call | flops 20000000000 | bytes 62914560 | tf_op jit(solution)/shard_map/pallas_call | solution.py:55
  3.3 0.5 %collective-permute-start = (f32[128,128]{1,0:T(8,128)S(1)}, f32[128,128]{1,0:T(8,128)S(1)}, u32[]{:S(2)}, u32[]{:S(2)}) collective-permute-start(f32[128,128]{1,0:T(8,128)S(1)} %get-tuple-element.12.own_ref), channel_id=1, source_target_pairs={{0,1},{1,0},{2,3},{3,2},{4,5},{5,4},{6,7},{7,6},{8,9},{9,8},{10,11... | collective-permute-start | bytes 196616 | tf_op jit(solution)/shard_map/ppermute | solution.py:237
  5.3 0.0 collective-permute-done.other_ref
  5.3 0.3 %shard_map.83 = f32[32,128]{1,0:T(8,128)S(1)} custom-call(s32[1]{0:T(128)S(6)} %copy.9.len_ref, f32[128,128]{1,0:T(8,128)S(1)} %get-tuple-element.12.own_ref, f32[128,128]{1,0:T(8,128)S(1)} %collective-permute-done.other_ref), custom_call_target="tpu_custom_call" | custom-call | tf_op jit(solution)/shard_map/pallas_call | solution.py:92
  5.6 3.6 %collective-permute-start.1 = (f32[1,32,128]{2,1,0:T(8,128)S(1)}, f32[1,32,128]{2,1,0:T(8,128)S(1)}, u32[]{:S(2)}, u32[]{:S(2)}) collective-permute-start(f32[1,32,128]{2,1,0:T(8,128)S(1)} %bitcast.5), channel_id=1, source_target_pairs={{0,9},{1,8},{2,11},{3,10},{4,13},{5,12},{6,15},{7,14},{8,1},{9,0},... | collective-permute-start | bytes 49160 | tf_op jit(solution)/shard_map/ppermute | solution.py:246
  9.1 0.0 slice-done
  9.2 0.0 slice-done.1
  9.2 0.0 copy-done
  9.2 0.0 copy-done.1
  9.2 1.9 %shard_map.84.refs_0_ = f32[2,128,128]{2,1,0:T(8,128)S(1)} custom-call(f32[1,32,128]{2,1,0:T(8,128)S(1)} %bitcast.6, s32[4]{0:T(128)S(1)} %copy-done.1, bf16[4,128,7168]{2,1,0:T(8,128)(2,1)S(1)} %bitcast.4, bf16[4,128,4096]{2,1,0:T(8,128)(2,1)S(1)} %copy-done, bf16[64,7168]{1,0:T(8,128)(2,1)S(1)} %get-tuple-element.13.bx_ref, ...), custom_call_target="tpu_custom_call" | custom-call | flops 369098752 | bytes 6291456 | tf_op jit(solution)/shard_map/pallas_call | solution.py:146
  11.1 0.0 collective-permute-done.1
  11.1 1.6 %collective-permute-start.3 = (f32[2,32,128]{2,1,0:T(8,128)S(1)}, f32[2,32,128]{2,1,0:T(8,128)S(1)}, u32[]{:S(2)}, u32[]{:S(2)}) collective-permute-start(f32[2,32,128]{2,1,0:T(8,128)S(1)} %pad_maximum_fusion.1.after_ref), channel_id=1, source_target_pairs={{0,5},{1,4},{2,7},{3,6},{4,1},{5,0},{6,3},{7,2},{8,13},{9,12},{10,... | collective-permute-start | bytes 98312 | tf_op jit(solution)/shard_map/ppermute | solution.py:246
  12.7 0.3 %collective-permute-start.2 = (f32[2,128,128]{2,1,0:T(8,128)S(1)}, f32[2,128,128]{2,1,0:T(8,128)S(1)}, u32[]{:S(2)}, u32[]{:S(2)}) collective-permute-start(f32[2,128,128]{2,1,0:T(8,128)S(1)} %shard_map.84.refs_0_), channel_id=1, source_target_pairs={{0,1},{1,0},{2,3},{3,2},{4,5},{5,4},{6,7},{7,6},{8,9},{9,8},{10,11... | collective-permute-start | bytes 393224 | tf_op jit(solution)/shard_map/ppermute | solution.py:237
  13.1 2.0 %shard_map.85.refs_2_ = f32[2,128,128]{2,1,0:T(8,128)S(1)} custom-call(f32[2,32,128]{2,1,0:T(8,128)S(1)} %pad_maximum_fusion.1.after_ref, s32[4]{0:T(128)S(1)} %copy-done.1, bf16[4,128,7168]{2,1,0:T(8,128)(2,1)S(1)} %bitcast.4, bf16[4,128,4096]{2,1,0:T(8,128)(2,1)S(1)} %copy-done, bf16[64,7168]{1,0:T(8,128)(2,1)S(1)} %get-tuple-element.13.bx_ref, ...), custom_call_target="tpu_custom_call" | custom-call | flops 369098752 | bytes 6291456 | tf_op jit(solution)/shard_map/pallas_call | solution.py:146
  15.1 0.0 collective-permute-done.3
  15.1 0.2 %collective-permute-start.4 = (f32[2,128,128]{2,1,0:T(8,128)S(1)}, f32[2,128,128]{2,1,0:T(8,128)S(1)}, u32[]{:S(2)}, u32[]{:S(2)}) collective-permute-start(f32[2,128,128]{2,1,0:T(8,128)S(1)} %shard_map.85.refs_2_), channel_id=1, source_target_pairs={{0,1},{1,0},{2,3},{3,2},{4,5},{5,4},{6,7},{7,6},{8,9},{9,8},{10,11... | collective-permute-start | bytes 393224 | tf_op jit(solution)/shard_map/ppermute | solution.py:237
  15.3 1.2 %collective-permute-start.5 = (f32[4,32,128]{2,1,0:T(8,128)S(1)}, f32[4,32,128]{2,1,0:T(8,128)S(1)}, u32[]{:S(2)}, u32[]{:S(2)}) collective-permute-start(f32[4,32,128]{2,1,0:T(8,128)S(1)} %pad_maximum_fusion.refs_0_), channel_id=1, source_target_pairs={{0,3},{1,2},{2,1},{3,0},{4,7},{5,6},{6,5},{7,4},{8,11},{9,10},{10,... | collective-permute-start | bytes 196616 | tf_op jit(solution)/shard_map/ppermute | solution.py:246
  16.5 0.0 collective-permute-done.2.refs_1_
  16.5 0.0 collective-permute-done.4.refs_3_
  16.5 1.2 %shard_map.86.unit_ref = f32[4,32,128]{2,1,0:T(8,128)S(1)} custom-call(s32[4]{0:T(128)S(1)} %copy-done.1, f32[2,128,128]{2,1,0:T(8,128)S(1)} %shard_map.84.refs_0_, f32[2,128,128]{2,1,0:T(8,128)S(1)} %collective-permute-done.2.refs_1_, f32[2,128,128]{2,1,0:T(8,128)S(1)} %shard_map.85.refs_2_, f32[2,128,128]{2,1,0:T(8,128)S(1)} %collective-permute-done.4.refs_3_), custom_call_target="tpu_custom_call" | custom-call | tf_op jit(solution)/shard_map/pallas_call | solution.py:185
  17.7 1.5 %collective-permute-done.5.refs_1_ = f32[4,32,128]{2,1,0:T(8,128)S(1)} collective-permute-done((f32[4,32,128]{2,1,0:T(8,128)S(1)}, f32[4,32,128]{2,1,0:T(8,128)S(1)}, u32[]{:S(2)}, u32[]{:S(2)}) %collective-permute-start.5) | collective-permute-done | bytes 65568 | tf_op jit(solution)/shard_map/ppermute | solution.py:246
  19.2 0.8 %shard_map.87 = f32[4,8]{1,0:T(4,128)} custom-call(f32[4,32,128]{2,1,0:T(8,128)S(1)} %shard_map.86.unit_ref, f32[4,32,128]{2,1,0:T(8,128)S(1)} %pad_maximum_fusion.refs_0_, f32[4,32,128]{2,1,0:T(8,128)S(1)} %collective-permute-done.5.refs_1_), custom_call_target="tpu_custom_call" | custom-call | tf_op jit(solution)/shard_map/pallas_call | solution.py:227
  (3 shorter events, 0.0 us)
Async XLA Ops:
  0.0 9.2 %slice-start = ((s8[7340032]{0:T(1024)(128)(4,1)}), s8[4194304]{0:T(1024)(128)(4,1)S(1)}, s32[]{:S(2)}) async-start(s8[7340032]{0:T(1024)(128)(4,1)} %bitcast.3), calls=%async_computation | async-start | bytes 8388608
  0.0 9.2 %slice-start.1 = ((s8[7340032]{0:T(1024)(128)(4,1)}), s8[3145728]{0:T(1024)(128)(4,1)S(1)}, s32[]{:S(2)}) async-start(s8[7340032]{0:T(1024)(128)(4,1)} %bitcast.3), calls=%async_computation.1 | async-start | bytes 6291456
  0.0 9.2 %copy-start = (bf16[4,128,4096]{2,1,0:T(8,128)(2,1)S(1)}, bf16[4,128,4096]{2,1,0:T(8,128)(2,1)}, u32[]{:S(2)}) copy-start(bf16[4,128,4096]{2,1,0:T(8,128)(2,1)} %g_ref.3) | copy-start | bytes 12582916
  0.0 9.2 %copy-start.1 = (s32[4]{0:T(128)S(1)}, s32[4]{0:T(128)}, u32[]{:S(2)}) copy-start(s32[4]{0:T(128)} %lens.5) | copy-start | bytes 52
  3.3 2.0 %collective-permute-start = (f32[128,128]{1,0:T(8,128)S(1)}, f32[128,128]{1,0:T(8,128)S(1)}, u32[]{:S(2)}, u32[]{:S(2)}) collective-permute-start(f32[128,128]{1,0:T(8,128)S(1)} %get-tuple-element.12.own_ref), channel_id=1, source_target_pairs={{0,1},{1,0},{2,3},{3,2},{4,5},{5,4},{6,7},{7,6},{8,9},{9,8},{10,11... | collective-permute-start | bytes 196616 | tf_op jit(solution)/shard_map/ppermute | solution.py:237
  5.6 5.5 %collective-permute-start.1 = (f32[1,32,128]{2,1,0:T(8,128)S(1)}, f32[1,32,128]{2,1,0:T(8,128)S(1)}, u32[]{:S(2)}, u32[]{:S(2)}) collective-permute-start(f32[1,32,128]{2,1,0:T(8,128)S(1)} %bitcast.5), channel_id=1, source_target_pairs={{0,9},{1,8},{2,11},{3,10},{4,13},{5,12},{6,15},{7,14},{8,1},{9,0},... | collective-permute-start | bytes 49160 | tf_op jit(solution)/shard_map/ppermute | solution.py:246
  11.1 3.9 %collective-permute-start.3 = (f32[2,32,128]{2,1,0:T(8,128)S(1)}, f32[2,32,128]{2,1,0:T(8,128)S(1)}, u32[]{:S(2)}, u32[]{:S(2)}) collective-permute-start(f32[2,32,128]{2,1,0:T(8,128)S(1)} %pad_maximum_fusion.1.after_ref), channel_id=1, source_target_pairs={{0,5},{1,4},{2,7},{3,6},{4,1},{5,0},{6,3},{7,2},{8,13},{9,12},{10,... | collective-permute-start | bytes 98312 | tf_op jit(solution)/shard_map/ppermute | solution.py:246
  12.7 3.7 %collective-permute-start.2 = (f32[2,128,128]{2,1,0:T(8,128)S(1)}, f32[2,128,128]{2,1,0:T(8,128)S(1)}, u32[]{:S(2)}, u32[]{:S(2)}) collective-permute-start(f32[2,128,128]{2,1,0:T(8,128)S(1)} %shard_map.84.refs_0_), channel_id=1, source_target_pairs={{0,1},{1,0},{2,3},{3,2},{4,5},{5,4},{6,7},{7,6},{8,9},{9,8},{10,11... | collective-permute-start | bytes 393224 | tf_op jit(solution)/shard_map/ppermute | solution.py:237
  15.1 1.4 %collective-permute-start.4 = (f32[2,128,128]{2,1,0:T(8,128)S(1)}, f32[2,128,128]{2,1,0:T(8,128)S(1)}, u32[]{:S(2)}, u32[]{:S(2)}) collective-permute-start(f32[2,128,128]{2,1,0:T(8,128)S(1)} %shard_map.85.refs_2_), channel_id=1, source_target_pairs={{0,1},{1,0},{2,3},{3,2},{4,5},{5,4},{6,7},{7,6},{8,9},{9,8},{10,11... | collective-permute-start | bytes 393224 | tf_op jit(solution)/shard_map/ppermute | solution.py:237
  15.3 3.9 %collective-permute-start.5 = (f32[4,32,128]{2,1,0:T(8,128)S(1)}, f32[4,32,128]{2,1,0:T(8,128)S(1)}, u32[]{:S(2)}, u32[]{:S(2)}) collective-permute-start(f32[4,32,128]{2,1,0:T(8,128)S(1)} %pad_maximum_fusion.refs_0_), channel_id=1, source_target_pairs={{0,3},{1,2},{2,1},{3,0},{4,7},{5,6},{6,5},{7,4},{8,11},{9,10},{10,... | collective-permute-start | bytes 196616 | tf_op jit(solution)/shard_map/ppermute | solution.py:246

commit v2 on v1

--- a/solution.py
+++ b/solution.py
@@ -10,7 +10,7 @@
 
 CHUNK = 2048
 TILE = 32
-REF_ROOM = 8 << 20
+REF_ROOM = 51_000_000
 ROLL_ROOM = 8 << 20
 EXACT = lax.Precision.HIGHEST
 
@@ -67,7 +67,7 @@
             pltpu.SemaphoreType.DMA((2, parts)),
         ],
         compiler_params=pltpu.CompilerParams(vmem_limit_bytes=REF_ROOM),
-        cost_estimate=pl.CostEstimate(flops=20_000_000_000, bytes_accessed=60 << 20, transcendentals=0),
+        cost_estimate=pl.CostEstimate(flops=20000000000, bytes_accessed=62914560, transcendentals=0),
     )(*(pltpu.with_memory_space_constraint(a, pltpu.HBM) for a in (x, g, bx, bg)))
 
 
@@ -96,6 +96,7 @@
         + [pl.BlockSpec(memory_space=pltpu.VMEM)] * 2,
         out_specs=pl.BlockSpec(memory_space=pltpu.VMEM),
         compiler_params=pltpu.CompilerParams(vmem_limit_bytes=8 << 20),
+        cost_estimate=pl.CostEstimate(flops=2000000000, bytes_accessed=6291456, transcendentals=0),
     )(length, own, other)
 
 
@@ -111,85 +112,74 @@
     return [
         sum(jnp.where(ranks[i] == place, jnp.int32(i), 0) for i in range(rolls))
         for place in range(rolls)
-    ], ranks
-
-
-def steps_of(length):
-    return (length + (STEP - 1)) // STEP
-
-
-def roll_kernel(places, after_ref, lens, x_ref, g_ref, bx_ref, bg_ref, z_ref):
+    ]
+
+
+def roll_kernel(places, earlier, *refs):
+    _, lens, x_ref, g_ref, bx_ref, bg_ref, z_ref = refs[earlier:]
     rolls, span, _ = x_ref.shape
-    numbers, _ = by_length(lens, rolls)
+    row = lens[...]
+    lens = [row[i] for i in range(rolls)]
+    numbers = by_length(lens, rolls)
     half = bg_ref.shape[0]
 
     @pl.loop(0, len(places))
     def _(slot):
         roll = sum(jnp.where(slot == k, numbers[p], 0) for k, p in enumerate(places))
-        need = (lens[roll] + (TILE - 1)) // TILE
+        need = (sum(jnp.where(roll == i, lens[i], 0) for i in range(rolls)) + (TILE - 1)) // TILE
         for tiles in range(1, span // TILE + 1):
 
             @pl.when(need == tiles)
             def _():
                 rows = pl.ds(0, tiles * TILE)
                 for k, (src, basis) in enumerate(((g_ref, bg_ref), (x_ref, bx_ref))):
-                    z_ref[slot, rows, k * half : (k + 1) * half] = times_basis(
+                    z_ref[roll, rows, k * half : (k + 1) * half] = times_basis(
                         src[roll, rows, :], basis[...]
                     )
 
 
-def project_rolls(places, after, x, g, bx, bg, lengths):
+def project_rolls(places, earlier, after, x, g, bx, bg, lengths):
     rolls, span, wide_x = x.shape
-    wide_g = g.shape[2]
-    count = len(places)
     held = pl.BlockSpec(memory_space=pltpu.VMEM)
-    return pl.pallas_call(
-        functools.partial(roll_kernel, places),
-        out_shape=jax.ShapeDtypeStruct((count, span, bx.shape[0] * 2), jnp.float32),
-        in_specs=[
-            pl.BlockSpec(memory_space=pl.ANY),
-            pl.BlockSpec(memory_space=pltpu.SMEM),
-            held, held, held, held,
-        ],
+    outside = pl.BlockSpec(memory_space=pl.ANY)
+    return pl.pallas_call(
+        functools.partial(roll_kernel, places, len(earlier)),
+        out_shape=jax.ShapeDtypeStruct((rolls, span, bx.shape[0] * 2), jnp.float32),
+        in_specs=[held] * len(earlier)
+        + [outside, held, held, held, held, held],
         out_specs=held,
+        input_output_aliases={0: 0} if earlier else {},
         compiler_params=pltpu.CompilerParams(vmem_limit_bytes=ROLL_ROOM),
         cost_estimate=pl.CostEstimate(
-            flops=2 * count * span * (wide_x + wide_g) * 64,
+            flops=2 * len(places) * span * (wide_x + g.shape[2]) * 64,
             bytes_accessed=6 << 20,
             transcendentals=0,
         ),
-    )(after, lengths, x, g, bx, bg)
-
-
-def units_kernel(shares, lens, *refs):
-    unit_ref = refs[-1]
-    rolls = lens.shape[0]
-    _, ranks = by_length(lens, rolls)
-    span = refs[0].shape[1]
-    for share, places in enumerate(shares):
-        own_ref, other_ref = refs[2 * share : 2 * share + 2]
-        for slot, place in enumerate(places):
-            roll = sum(jnp.where(ranks[i] == place, jnp.int32(i), 0) for i in range(rolls))
-            z = own_ref[slot] + other_ref[slot]
-            keep = lax.broadcasted_iota(jnp.int32, z.shape, 0) < lens[roll]
-            sketch = sketch_of(jnp.where(keep, z, 0.0))
-            square = jnp.sum(sketch * sketch, axis=(0, 1), keepdims=True)
-            size = sketch.shape[0] * sketch.shape[1]
-            unit_ref[roll] = sketch / (jnp.sqrt(square / size + 1e-6) * math.sqrt(size))
-
-
-def roll_units(shares, lengths, parts):
+    )(*earlier, after, lengths, x, g, bx, bg)
+
+
+def units_kernel(lens, own_ref, other_ref, unit_ref):
+    row = lens[...]
+    rolls = [row[i] for i in range(lens.shape[0])]
+    for roll, length in enumerate(rolls):
+        z = own_ref[roll] + other_ref[roll]
+        keep = lax.broadcasted_iota(jnp.int32, z.shape, 0) < length
+        sketch = sketch_of(jnp.where(keep, z, 0.0))
+        square = jnp.sum(sketch * sketch, axis=(0, 1), keepdims=True)
+        size = sketch.shape[0] * sketch.shape[1]
+        unit_ref[roll] = sketch / (jnp.sqrt(square / size + 1e-6) * math.sqrt(size))
+
+
+def roll_units(lengths, own, other):
     rolls = lengths.shape[0]
-    half = parts[0][0].shape[2] // 2
-    flat = [z for pair in parts for z in pair]
-    return pl.pallas_call(
-        functools.partial(units_kernel, shares),
+    half = own.shape[2] // 2
+    return pl.pallas_call(
+        units_kernel,
         out_shape=jax.ShapeDtypeStruct((rolls, half // 2, half * 2), jnp.float32),
-        in_specs=[pl.BlockSpec(memory_space=pltpu.SMEM)]
-        + [pl.BlockSpec(memory_space=pltpu.VMEM)] * len(flat),
+        in_specs=[pl.BlockSpec(memory_space=pltpu.VMEM)] * 3,
         out_specs=pl.BlockSpec(memory_space=pltpu.VMEM),
         compiler_params=pltpu.CompilerParams(vmem_limit_bytes=8 << 20),
-    )(lengths, *flat)
+    )(lengths, own, other)
 
 
 def score_kernel(order, dp_axis, unit_ref, *refs):
@@ -258,17 +248,20 @@
     held = sketch[None]
     order = [0]
     bits = [1 << k for k in range(devices.bit_length() - 1)][::-1]
-    parts = []
+    roll_z = ()
     for step, bit in enumerate(bits):
+        last = step == len(bits) - 1
+        if last:
+            held, z = lax.optimization_barrier((held, z))
         got = from_chip(held, bit, devices, cores)
         if step < len(shares):
-            z = project_rolls(shares[step], held, roll_inputs, roll_grads, bx, bg, roll_lengths)
+            z = project_rolls(shares[step], roll_z, held, roll_inputs, roll_grads, bx, bg, roll_lengths)
             got, z = lax.optimization_barrier((got, z))
-            parts.append((z, other_core(z)))
+            roll_z = (z,)
         order = order + [k ^ bit for k in order]
-        if step < len(bits) - 1:
+        if not last:
             held = jnp.concatenate([held, got], axis=0)
-    units = roll_units(shares, roll_lengths, parts)
+    units = roll_units(roll_lengths, z, other_core(z))
     return score(units, (held, got), tuple(order))
 
 

time: 20.1 us -> 19.2 us (0.955)
  Pallas kernels: 9.53 us -> 8.25 us
  waiting for transfers between devices: 1.55 us -> 2.78 us
  starting transfers between devices: 7.45 us -> 6.98 us
  between operations: 1.5 us -> 1.11 us
    pallas_call x3, Pallas kernels: 5.09 us -> 3.82 us  [the longest x2 2.98 us: project_rolls(): pl.pallas_call(functools.partial(roll_kernel, places, len(earlier)), out_...]
    ppermute x3, waiting for transfers between devices: 1.54 us -> 2.57 us  [from_chip(): return lax.ppermute(value, ('dp', 'tensor'), pairs)]
    ppermute x3 -> x2, starting transfers between devices: 1.09 us -> 0.63 us  [other_core(): return lax.ppermute(value, 'tensor', [(0, 1), (1, 0)])]
  transfers between devices with their start and end apart: 6 -> 5, of which waited for: 1 -> 3; matrix products, arithmetic and copies ran while one was open for 0% -> 0% of each run, Pallas kernels for 25% -> 20%
where the time goes in v2:
time: 19.2 us
  Pallas kernels  8.25 us (43%)
  starting transfers between devices  6.98 us (36%)
  waiting for transfers between devices  2.78 us (14%)
  between operations  1.11 us (6%)
    ppermute x3, starting transfers between devices, from_chip(): return lax.ppermute(value, ('dp', 'tensor'), pairs)  6.35 us
    pallas_call x1, Pallas kernels, project_ref(): pl.pallas_call(ref_kernel, out_shape=(jax.ShapeDtypeStruct((span, bx.shap...  3.27 us
    pallas_call x2, Pallas kernels, project_rolls(): pl.pallas_call(functools.partial(roll_kernel, places, len(earlier)), out_...  2.98 us
    ppermute x3, waiting for transfers between devices, from_chip(): return lax.ppermute(value, ('dp', 'tensor'), pairs)  2.57 us
    pallas_call x1, Pallas kernels, score(): pl.pallas_call(functools.partial(score_kernel, order, 'dp'), out_shape=ja...  0.84 us
    pallas_call x1, Pallas kernels, roll_units(): pl.pallas_call(units_kernel, out_shape=jax.ShapeDtypeStruct((rolls, half...  0.84 us
    ppermute x2, starting transfers between devices, other_core(): return lax.ppermute(value, 'tensor', [(0, 1), (1, 0)])  0.63 us
  transfers between devices with their start and end apart: 5, of which 3 were waited for; matrix products, arithmetic and copies ran while one was open for 0% of the time, Pallas kernels for 20%

profile of v2, /device:TPU:0, one launch (start us, length us, event | category | flops | bytes accessed | tf_op | source)
XLA Modules:
  0.0 19.2 jit_solution(10411057507639304914)
XLA Ops:
  0.0 0.0 slice-start
  0.0 0.0 slice-start.1
  0.0 3.3 %shard_map.82 = (f32[128,128]{1,0:T(8,128)S(1)}, bf16[64,7168]{1,0:T(8,128)(2,1)S(1)}, bf16[64,4096]{1,0:T(8,128)(2,1)S(1)}) custom-call(bf16[1,128,7168]{2,1,0:T(8,128)(2,1)} %x_hbm.1, bf16[1,128,4096]{2,1,0:T(8,128)(2,1)} %g_hbm.1, bf16[64,7168]{1,0:T(8,128)(2,1)} %bitcast.9, bf16[64,4096]{1,0:T(8,128)(2,1)} %bitcast.10), custom_call_target="tpu_custom_call" | custom-call | flops 20000000000 | bytes 62914560 | tf_op jit(solution)/shard_map/pallas_call | solution.py:55
  3.3 0.0 copy-start
  3.3 0.0 copy-start.1
  3.3 0.5 %collective-permute-start = (f32[128,128]{1,0:T(8,128)S(1)}, f32[128,128]{1,0:T(8,128)S(1)}, u32[]{:S(2)}, u32[]{:S(2)}) collective-permute-start(f32[128,128]{1,0:T(8,128)S(1)} %get-tuple-element.14.own_ref), channel_id=1, source_target_pairs={{0,1},{1,0},{2,3},{3,2},{4,5},{5,4},{6,7},{7,6},{8,9},{9,8},{10,11... | collective-permute-start | bytes 196616 | tf_op jit(solution)/shard_map/ppermute | solution.py:227
  4.9 0.0 collective-permute-done.other_ref
  4.9 0.3 %shard_map.83 = f32[32,128]{1,0:T(8,128)S(1)} custom-call(s32[1]{0:T(128)S(6)} %copy.11.len_ref, f32[128,128]{1,0:T(8,128)S(1)} %get-tuple-element.14.own_ref, f32[128,128]{1,0:T(8,128)S(1)} %collective-permute-done.other_ref), custom_call_target="tpu_custom_call" | custom-call | flops 2000000000 | bytes 6291456 | tf_op jit(solution)/shard_map/pallas_call | solution.py:92
  5.2 3.8 %collective-permute-start.1 = (f32[1,32,128]{2,1,0:T(8,128)S(1)}, f32[1,32,128]{2,1,0:T(8,128)S(1)}, u32[]{:S(2)}, u32[]{:S(2)}) collective-permute-start(f32[1,32,128]{2,1,0:T(8,128)S(1)} %bitcast.5), channel_id=1, source_target_pairs={{0,9},{1,8},{2,11},{3,10},{4,13},{5,12},{6,15},{7,14},{8,1},{9,0},... | collective-permute-start | bytes 49160 | tf_op jit(solution)/shard_map/ppermute | solution.py:236
  9.0 0.0 slice-done
  9.0 0.0 slice-done.1
  9.0 0.0 copy-done
  9.0 0.0 copy-done.1
  9.1 1.7 %shard_map.84.refs_0_ = f32[4,128,128]{2,1,0:T(8,128)S(1)} custom-call(f32[1,32,128]{2,1,0:T(8,128)S(1)} %bitcast.6, s32[4]{0:T(128)S(1)} %copy-done.1, bf16[4,128,7168]{2,1,0:T(8,128)(2,1)S(1)} %bitcast.4, bf16[4,128,4096]{2,1,0:T(8,128)(2,1)S(1)} %copy-done, bf16[64,7168]{1,0:T(8,128)(2,1)S(1)} %get-tuple-element.15.refs_4_.refs_5_, ...), custom_call_target="tpu_custom_call" | custom-call | flops 369098752 | bytes 6291456 | tf_op jit(solution)/shard_map/pallas_call | solution.py:145
  10.7 0.0 collective-permute-done.1
  10.8 1.3 %collective-permute-start.2 = (f32[2,32,128]{2,1,0:T(8,128)S(1)}, f32[2,32,128]{2,1,0:T(8,128)S(1)}, u32[]{:S(2)}, u32[]{:S(2)}) collective-permute-start(f32[2,32,128]{2,1,0:T(8,128)S(1)} %pad_maximum_fusion.1.refs_1_), channel_id=1, source_target_pairs={{0,5},{1,4},{2,7},{3,6},{4,1},{5,0},{6,3},{7,2},{8,13},{9,12},{10,... | collective-permute-start | bytes 98312 | tf_op jit(solution)/shard_map/ppermute | solution.py:236
  12.1 1.3 %shard_map.85.own_ref = f32[4,128,128]{2,1,0:T(8,128)S(1)} custom-call(f32[4,128,128]{2,1,0:T(8,128)S(1)} %shard_map.84.refs_0_, f32[2,32,128]{2,1,0:T(8,128)S(1)} %pad_maximum_fusion.1.refs_1_, s32[4]{0:T(128)S(1)} %copy-done.1, bf16[4,128,7168]{2,1,0:T(8,128)(2,1)S(1)} %bitcast.4, ...), custom_call_target="tpu_custom_call", output_to_operand_aliasing={{}: (0, {})} | custom-call | flops 369098752 | bytes 6291456 | tf_op jit(solution)/shard_map/pallas_call | solution.py:145
  13.4 0.9 %collective-permute-done.2 = f32[2,32,128]{2,1,0:T(8,128)S(1)} collective-permute-done((f32[2,32,128]{2,1,0:T(8,128)S(1)}, f32[2,32,128]{2,1,0:T(8,128)S(1)}, u32[]{:S(2)}, u32[]{:S(2)}) %collective-permute-start.2) | collective-permute-done | bytes 32800 | tf_op jit(solution)/shard_map/ppermute | solution.py:236
  14.3 0.1 collective-permute-start.3
  14.4 1.2 %collective-permute-start.4 = (f32[4,32,128]{2,1,0:T(8,128)S(1)}, f32[4,32,128]{2,1,0:T(8,128)S(1)}, u32[]{:S(2)}, u32[]{:S(2)}) collective-permute-start(f32[4,32,128]{2,1,0:T(8,128)S(1)} %pad_maximum_fusion.refs_0_), channel_id=1, source_target_pairs={{0,3},{1,2},{2,1},{3,0},{4,7},{5,6},{6,5},{7,4},{8,11},{9,10},{10,... | collective-permute-start | bytes 196616 | tf_op jit(solution)/shard_map/ppermute | solution.py:236
  15.6 0.2 %collective-permute-done.3.other_ref = f32[4,128,128]{2,1,0:T(8,128)S(1)} collective-permute-done((f32[4,128,128]{2,1,0:T(8,128)S(1)}, f32[4,128,128]{2,1,0:T(8,128)S(1)}, u32[]{:S(2)}, u32[]{:S(2)}) %collective-permute-start.3) | collective-permute-done | bytes 262176 | tf_op jit(solution)/shard_map/ppermute | solution.py:227
  15.8 0.8 %shard_map.86.unit_ref = f32[4,32,128]{2,1,0:T(8,128)S(1)} custom-call(s32[4]{0:T(128)S(1)} %copy-done.1, f32[4,128,128]{2,1,0:T(8,128)S(1)} %shard_map.85.own_ref, f32[4,128,128]{2,1,0:T(8,128)S(1)} %collective-permute-done.3.other_ref), custom_call_target="tpu_custom_call" | custom-call | tf_op jit(solution)/shard_map/pallas_call | solution.py:176
  16.6 1.7 %collective-permute-done.4.refs_1_ = f32[4,32,128]{2,1,0:T(8,128)S(1)} collective-permute-done((f32[4,32,128]{2,1,0:T(8,128)S(1)}, f32[4,32,128]{2,1,0:T(8,128)S(1)}, u32[]{:S(2)}, u32[]{:S(2)}) %collective-permute-start.4) | collective-permute-done | bytes 65568 | tf_op jit(solution)/shard_map/ppermute | solution.py:236
  18.3 0.8 %shard_map.87 = f32[4,8]{1,0:T(4,128)} custom-call(f32[4,32,128]{2,1,0:T(8,128)S(1)} %shard_map.86.unit_ref, f32[4,32,128]{2,1,0:T(8,128)S(1)} %pad_maximum_fusion.refs_0_, f32[4,32,128]{2,1,0:T(8,128)S(1)} %collective-permute-done.4.refs_1_), custom_call_target="tpu_custom_call" | custom-call | tf_op jit(solution)/shard_map/pallas_call | solution.py:217
  (3 shorter events, 0.0 us)
Async XLA Ops:
  0.0 9.0 %slice-start = ((s8[7340032]{0:T(1024)(128)(4,1)}), s8[4194304]{0:T(1024)(128)(4,1)S(1)}, s32[]{:S(2)}) async-start(s8[7340032]{0:T(1024)(128)(4,1)} %bitcast.3), calls=%async_computation | async-start | bytes 8388608
  0.0 9.0 %slice-start.1 = ((s8[7340032]{0:T(1024)(128)(4,1)}), s8[3145728]{0:T(1024)(128)(4,1)S(1)}, s32[]{:S(2)}) async-start(s8[7340032]{0:T(1024)(128)(4,1)} %bitcast.3), calls=%async_computation.1 | async-start | bytes 6291456
  3.3 5.8 %copy-start = (bf16[4,128,4096]{2,1,0:T(8,128)(2,1)S(1)}, bf16[4,128,4096]{2,1,0:T(8,128)(2,1)}, u32[]{:S(2)}) copy-start(bf16[4,128,4096]{2,1,0:T(8,128)(2,1)} %refs_4_.1) | copy-start | bytes 12582916
  3.3 5.8 %copy-start.1 = (s32[4]{0:T(128)S(1)}, s32[4]{0:T(128)}, u32[]{:S(2)}) copy-start(s32[4]{0:T(128)} %lens.1) | copy-start | bytes 52
  3.3 1.6 %collective-permute-start = (f32[128,128]{1,0:T(8,128)S(1)}, f32[128,128]{1,0:T(8,128)S(1)}, u32[]{:S(2)}, u32[]{:S(2)}) collective-permute-start(f32[128,128]{1,0:T(8,128)S(1)} %get-tuple-element.14.own_ref), channel_id=1, source_target_pairs={{0,1},{1,0},{2,3},{3,2},{4,5},{5,4},{6,7},{7,6},{8,9},{9,8},{10,11... | collective-permute-start | bytes 196616 | tf_op jit(solution)/shard_map/ppermute | solution.py:227
  5.2 5.5 %collective-permute-start.1 = (f32[1,32,128]{2,1,0:T(8,128)S(1)}, f32[1,32,128]{2,1,0:T(8,128)S(1)}, u32[]{:S(2)}, u32[]{:S(2)}) collective-permute-start(f32[1,32,128]{2,1,0:T(8,128)S(1)} %bitcast.5), channel_id=1, source_target_pairs={{0,9},{1,8},{2,11},{3,10},{4,13},{5,12},{6,15},{7,14},{8,1},{9,0},... | collective-permute-start | bytes 49160 | tf_op jit(solution)/shard_map/ppermute | solution.py:236
  10.8 3.5 %collective-permute-start.2 = (f32[2,32,128]{2,1,0:T(8,128)S(1)}, f32[2,32,128]{2,1,0:T(8,128)S(1)}, u32[]{:S(2)}, u32[]{:S(2)}) collective-permute-start(f32[2,32,128]{2,1,0:T(8,128)S(1)} %pad_maximum_fusion.1.refs_1_), channel_id=1, source_target_pairs={{0,5},{1,4},{2,7},{3,6},{4,1},{5,0},{6,3},{7,2},{8,13},{9,12},{10,... | collective-permute-start | bytes 98312 | tf_op jit(solution)/shard_map/ppermute | solution.py:236
  14.3 1.5 %collective-permute-start.3 = (f32[4,128,128]{2,1,0:T(8,128)S(1)}, f32[4,128,128]{2,1,0:T(8,128)S(1)}, u32[]{:S(2)}, u32[]{:S(2)}) collective-permute-start(f32[4,128,128]{2,1,0:T(8,128)S(1)} %shard_map.85.own_ref), channel_id=1, source_target_pairs={{0,1},{1,0},{2,3},{3,2},{4,5},{5,4},{6,7},{7,6},{8,9},{9,8},{10,11... | collective-permute-start | bytes 786440 | tf_op jit(solution)/shard_map/ppermute | solution.py:227
  14.4 3.9 %collective-permute-start.4 = (f32[4,32,128]{2,1,0:T(8,128)S(1)}, f32[4,32,128]{2,1,0:T(8,128)S(1)}, u32[]{:S(2)}, u32[]{:S(2)}) collective-permute-start(f32[4,32,128]{2,1,0:T(8,128)S(1)} %pad_maximum_fusion.refs_0_), channel_id=1, source_target_pairs={{0,3},{1,2},{2,1},{3,0},{4,7},{5,6},{6,5},{7,4},{8,11},{9,10},{10,... | collective-permute-start | bytes 196616 | tf_op jit(solution)/shard_map/ppermute | solution.py:236

commit v3 on v2

--- a/solution.py
+++ b/solution.py
@@ -11,8 +11,11 @@
 CHUNK = 2048
 TILE = 32
 REF_ROOM = 51_000_000
-ROLL_ROOM = 8 << 20
+ROLL_ROOM = 20 << 20
 EXACT = lax.Precision.HIGHEST
+ROOM_FOR_PREFETCH = pl.CostEstimate(
+    flops=20_000_000_000, bytes_accessed=60 << 20, transcendentals=0
+)
 
 
 def columns(width):
@@ -67,7 +70,7 @@
             pltpu.SemaphoreType.DMA((2, parts)),
         ],
         compiler_params=pltpu.CompilerParams(vmem_limit_bytes=REF_ROOM),
-        cost_estimate=pl.CostEstimate(flops=20000000000, bytes_accessed=62914560, transcendentals=0),
+        cost_estimate=ROOM_FOR_PREFETCH,
     )(*(pltpu.with_memory_space_constraint(a, pltpu.HBM) for a in (x, g, bx, bg)))
 
 
@@ -96,37 +99,20 @@
         + [pl.BlockSpec(memory_space=pltpu.VMEM)] * 2,
         out_specs=pl.BlockSpec(memory_space=pltpu.VMEM),
         compiler_params=pltpu.CompilerParams(vmem_limit_bytes=8 << 20),
-        cost_estimate=pl.CostEstimate(flops=2000000000, bytes_accessed=6291456, transcendentals=0),
+        cost_estimate=ROOM_FOR_PREFETCH,
     )(length, own, other)
 
 
-def by_length(lens, rolls):
-    ranks = []
-    for i in range(rolls):
-        rank = jnp.int32(0)
-        for j in range(rolls):
-            if j != i:
-                ahead = lens[j] >= lens[i] if j < i else lens[j] > lens[i]
-                rank = rank + ahead.astype(jnp.int32)
-        ranks.append(rank)
-    return [
-        sum(jnp.where(ranks[i] == place, jnp.int32(i), 0) for i in range(rolls))
-        for place in range(rolls)
-    ]
-
-
-def roll_kernel(places, earlier, *refs):
-    _, lens, x_ref, g_ref, bx_ref, bg_ref, z_ref = refs[earlier:]
+def roll_kernel(after_ref, len_ref, x_ref, g_ref, bx_ref, bg_ref, z_ref):
     rolls, span, _ = x_ref.shape
-    row = lens[...]
+    row = len_ref[...]
     lens = [row[i] for i in range(rolls)]
-    numbers = by_length(lens, rolls)
     half = bg_ref.shape[0]
 
-    @pl.loop(0, len(places))
-    def _(slot):
-        roll = sum(jnp.where(slot == k, numbers[p], 0) for k, p in enumerate(places))
-        need = (sum(jnp.where(roll == i, lens[i], 0) for i in range(rolls)) + (TILE - 1)) // TILE
+    @pl.loop(0, rolls)
+    def _(roll):
+        length = sum(jnp.where(roll == i, lens[i], 0) for i in range(rolls))
+        need = (length + (TILE - 1)) // TILE
         for tiles in range(1, span // TILE + 1):
 
             @pl.when(need == tiles)
@@ -138,24 +124,22 @@
                     )
 
 
-def project_rolls(places, earlier, after, x, g, bx, bg, lengths):
-    rolls, span, wide_x = x.shape
+def project_rolls(operands):
+    rolls, span, wide_x = operands[2].shape
+    wide_g, width = operands[3].shape[2], operands[4].shape[0] * 2
     held = pl.BlockSpec(memory_space=pltpu.VMEM)
-    outside = pl.BlockSpec(memory_space=pl.ANY)
-    return pl.pallas_call(
-        functools.partial(roll_kernel, places, len(earlier)),
-        out_shape=jax.ShapeDtypeStruct((rolls, span, bx.shape[0] * 2), jnp.float32),
-        in_specs=[held] * len(earlier)
-        + [outside, held, held, held, held, held],
+    return pl.pallas_call(
+        roll_kernel,
+        out_shape=jax.ShapeDtypeStruct((rolls, span, width), jnp.float32),
+        in_specs=[pl.BlockSpec(memory_space=pl.ANY)] + [held] * 5,
         out_specs=held,
-        input_output_aliases={0: 0} if earlier else {},
         compiler_params=pltpu.CompilerParams(vmem_limit_bytes=ROLL_ROOM),
         cost_estimate=pl.CostEstimate(
-            flops=2 * len(places) * span * (wide_x + g.shape[2]) * 64,
-            bytes_accessed=6 << 20,
+            flops=rolls * span * (wide_x + wide_g) * width,
+            bytes_accessed=12 << 20,
             transcendentals=0,
         ),
-    )(*earlier, after, lengths, x, g, bx, bg)
+    )(*operands)
 
 
 def units_kernel(lens, own_ref, other_ref, unit_ref):
@@ -241,28 +225,23 @@
     roll_lengths, ref_lengths,
 ):
     bx, bg = in_basis.T, out_basis.T
-    shares = ((0, 3), (1, 2))
     ref_z, bx, bg = project_ref(ref_inputs, ref_grads, bx, bg)
     sketch = ref_sketch(ref_lengths, ref_z, other_core(ref_z))
 
     held = sketch[None]
     order = [0]
-    bits = [1 << k for k in range(devices.bit_length() - 1)][::-1]
-    roll_z = ()
-    for step, bit in enumerate(bits):
-        last = step == len(bits) - 1
-        if last:
-            held, z = lax.optimization_barrier((held, z))
-        got = from_chip(held, bit, devices, cores)
-        if step < len(shares):
-            z = project_rolls(shares[step], roll_z, held, roll_inputs, roll_grads, bx, bg, roll_lengths)
-            got, z = lax.optimization_barrier((got, z))
-            roll_z = (z,)
+    bits = [1 << k for k in range(devices.bit_length() - 1)]
+    turns = (bits[1], bits[2], bits[1] ^ bits[2])
+    got = [from_chip(held, turn, devices, cores) for turn in turns]
+    z = project_rolls((held, roll_lengths, roll_inputs, roll_grads, bx, bg))
+    *got, z = lax.optimization_barrier((*got, z))
+    order = order + [k ^ turn for turn in turns for k in order]
+    for bit in bits[:1] + bits[3:]:
+        held = jnp.concatenate([held, *got], axis=0)
+        got = [from_chip(held, bit, devices, cores)]
         order = order + [k ^ bit for k in order]
-        if not last:
-            held = jnp.concatenate([held, got], axis=0)
     units = roll_units(roll_lengths, z, other_core(z))
-    return score(units, (held, got), tuple(order))
+    return score(units, (held, *got), tuple(order))
 
 
 def solution(mesh):

time: 19.2 us -> 19.1 us (level)
  starting transfers between devices: 6.98 us -> 7.45 us
  between operations: 1.11 us -> 0.87 us
  waiting for transfers between devices: 2.78 us -> 2.55 us
  Pallas kernels: 8.25 us -> 8.03 us
    ppermute x2, starting transfers between devices: 0.63 us -> 0.87 us  [other_core(): return lax.ppermute(value, 'tensor', [(0, 1), (1, 0)])]
    ppermute x3 -> x4, starting transfers between devices: 6.35 us -> 6.59 us  [from_chip(): return lax.ppermute(value, ('dp', 'tensor'), pairs)]
    ppermute x3 -> x4, waiting for transfers between devices: 2.57 us -> 2.49 us  [from_chip(): return lax.ppermute(value, ('dp', 'tensor'), pairs)]
    pallas_call x2 -> x1, Pallas kernels: 2.98 us -> 2.91 us  [project_rolls(): pl.pallas_call(roll_kernel, out_shape=jax.ShapeDtypeStruct((rolls, span,...]
  transfers between devices with their start and end apart: 5 -> 6, of which waited for: 3 -> 3; matrix products, arithmetic and copies ran while one was open for 0% -> 0% of each run, Pallas kernels for 20% -> 20%
where the time goes in v3:
time: 19.1 us; the launch traced here: 18.9 us
  Pallas kernels  8.03 us (42%)
  starting transfers between devices  7.45 us (39%)
  waiting for transfers between devices  2.55 us (13%)
  between operations  0.87 us (5%)
    ppermute x4, starting transfers between devices, from_chip(): return lax.ppermute(value, ('dp', 'tensor'), pairs)  6.59 us
    pallas_call x1, Pallas kernels, project_ref(): pl.pallas_call(ref_kernel, out_shape=(jax.ShapeDtypeStruct((span, bx.shap...  3.12 us
    pallas_call x1, Pallas kernels, project_rolls(): pl.pallas_call(roll_kernel, out_shape=jax.ShapeDtypeStruct((rolls, span,...  2.91 us
    ppermute x4, waiting for transfers between devices, from_chip(): return lax.ppermute(value, ('dp', 'tensor'), pairs)  2.49 us
    ppermute x2, starting transfers between devices, other_core(): return lax.ppermute(value, 'tensor', [(0, 1), (1, 0)])  0.87 us
    pallas_call x1, Pallas kernels, score(): pl.pallas_call(functools.partial(score_kernel, order, 'dp'), out_shape=ja...  0.84 us
    pallas_call x1, Pallas kernels, roll_units(): pl.pallas_call(units_kernel, out_shape=jax.ShapeDtypeStruct((rolls, half...  0.84 us
  transfers between devices with their start and end apart: 6, of which 3 were waited for; matrix products, arithmetic and copies ran while one was open for 0% of the time, Pallas kernels for 20%

profile of v3, /device:TPU:0, one launch (start us, length us, event | category | flops | bytes accessed | tf_op | source)
XLA Modules:
  0.0 18.9 jit_solution(1994767221774550732)
XLA Ops:
  0.0 3.1 %shard_map.82 = (f32[128,128]{1,0:T(8,128)S(1)}, bf16[64,7168]{1,0:T(8,128)(2,1)S(1)}, bf16[64,4096]{1,0:T(8,128)(2,1)S(1)}) custom-call(bf16[1,128,7168]{2,1,0:T(8,128)(2,1)} %x_hbm.1, bf16[1,128,4096]{2,1,0:T(8,128)(2,1)} %g_hbm.1, bf16[64,7168]{1,0:T(8,128)(2,1)} %bitcast.10, bf16[64,4096]{1,0:T(8,128)(2,1)} %bitcast.11), custom_call_target="tpu_custom_call" | custom-call | flops 20000000000 | bytes 62914560 | tf_op jit(solution)/shard_map/pallas_call | solution.py:58
  3.1 0.5 %collective-permute-start = (f32[128,128]{1,0:T(8,128)S(1)}, f32[128,128]{1,0:T(8,128)S(1)}, u32[]{:S(2)}, u32[]{:S(2)}) collective-permute-start(f32[128,128]{1,0:T(8,128)S(1)} %get-tuple-element.12.own_ref), channel_id=1, source_target_pairs={{0,1},{1,0},{2,3},{3,2},{4,5},{5,4},{6,7},{7,6},{8,9},{9,8},{10,11... | collective-permute-start | bytes 196616 | tf_op jit(solution)/shard_map/ppermute | solution.py:211
  3.6 0.0 slice-start
  4.4 0.0 slice-start.1
  4.5 0.0 copy-start
  4.5 0.0 copy-start.1
  4.5 0.1 collective-permute-done.other_ref
  4.5 0.3 %shard_map.83 = f32[32,128]{1,0:T(8,128)S(1)} custom-call(s32[1]{0:T(128)S(6)} %copy.9.len_ref, f32[128,128]{1,0:T(8,128)S(1)} %get-tuple-element.12.own_ref, f32[128,128]{1,0:T(8,128)S(1)} %collective-permute-done.other_ref), custom_call_target="tpu_custom_call" | custom-call | flops 20000000000 | bytes 62914560 | tf_op jit(solution)/shard_map/pallas_call | solution.py:95
  4.9 4.7 %collective-permute-start.3 = (f32[1,32,128]{2,1,0:T(8,128)S(1)}, f32[1,32,128]{2,1,0:T(8,128)S(1)}, u32[]{:S(2)}, u32[]{:S(2)}) collective-permute-start(f32[1,32,128]{2,1,0:T(8,128)S(1)} %bitcast.5), channel_id=1, source_target_pairs={{0,13},{1,12},{2,15},{3,14},{4,9},{5,8},{6,11},{7,10},{8,5},{9,4},... | collective-permute-start | bytes 49160 | tf_op jit(solution)/shard_map/ppermute | solution.py:220
  9.6 0.0 collective-permute-start.2
  9.6 0.6 %collective-permute-start.1 = (f32[1,32,128]{2,1,0:T(8,128)S(1)}, f32[1,32,128]{2,1,0:T(8,128)S(1)}, u32[]{:S(2)}, u32[]{:S(2)}) collective-permute-start(f32[1,32,128]{2,1,0:T(8,128)S(1)} %bitcast.7), channel_id=1, source_target_pairs={{0,5},{1,4},{2,7},{3,6},{4,1},{5,0},{6,3},{7,2},{8,13},{9,12},{10,... | collective-permute-start | bytes 49160 | tf_op jit(solution)/shard_map/ppermute | solution.py:220
  10.2 0.0 slice-done
  10.2 0.0 slice-done.1
  10.2 0.0 copy-done
  10.2 0.0 copy-done.1
  10.2 2.9 %shard_map.84.own_ref = f32[4,128,128]{2,1,0:T(8,128)S(1)} custom-call(f32[1,32,128]{2,1,0:T(8,128)S(1)} %bitcast.8, s32[4]{0:T(128)S(1)} %copy-done.1, bf16[4,128,7168]{2,1,0:T(8,128)(2,1)S(1)} %bitcast.4, bf16[4,128,4096]{2,1,0:T(8,128)(2,1)S(1)} %copy-done, bf16[64,7168]{1,0:T(8,128)(2,1)S(1)} %get-tuple-element.13.bx_ref, ...), custom_call_target="tpu_custom_call" | custom-call | flops 738197504 | bytes 12582912 | tf_op jit(solution)/shard_map/pallas_call | solution.py:131
  13.1 0.0 collective-permute-done.3
  13.2 0.5 %collective-permute-done.2 = f32[1,32,128]{2,1,0:T(8,128)S(1)} collective-permute-done((f32[1,32,128]{2,1,0:T(8,128)S(1)}, f32[1,32,128]{2,1,0:T(8,128)S(1)}, u32[]{:S(2)}, u32[]{:S(2)}) %collective-permute-start.2) | collective-permute-done | bytes 16416 | tf_op jit(solution)/shard_map/ppermute | solution.py:220
  13.7 0.0 collective-permute-done.1
  13.7 0.4 %collective-permute-start.4 = (f32[4,128,128]{2,1,0:T(8,128)S(1)}, f32[4,128,128]{2,1,0:T(8,128)S(1)}, u32[]{:S(2)}, u32[]{:S(2)}) collective-permute-start(f32[4,128,128]{2,1,0:T(8,128)S(1)} %shard_map.84.own_ref), channel_id=1, source_target_pairs={{0,1},{1,0},{2,3},{3,2},{4,5},{5,4},{6,7},{7,6},{8,9},{9,8},{10,11... | collective-permute-start | bytes 786440 | tf_op jit(solution)/shard_map/ppermute | solution.py:211
  14.0 1.2 %collective-permute-start.5 = (f32[4,32,128]{2,1,0:T(8,128)S(1)}, f32[4,32,128]{2,1,0:T(8,128)S(1)}, u32[]{:S(2)}, u32[]{:S(2)}) collective-permute-start(f32[4,32,128]{2,1,0:T(8,128)S(1)} %pad_maximum_fusion.refs_0_), channel_id=1, source_target_pairs={{0,3},{1,2},{2,1},{3,0},{4,7},{5,6},{6,5},{7,4},{8,11},{9,10},{10,... | collective-permute-start | bytes 196616 | tf_op jit(solution)/shard_map/ppermute | solution.py:220
  15.3 0.0 collective-permute-done.4.other_ref
  15.3 0.8 %shard_map.85.unit_ref = f32[4,32,128]{2,1,0:T(8,128)S(1)} custom-call(s32[4]{0:T(128)S(1)} %copy-done.1, f32[4,128,128]{2,1,0:T(8,128)S(1)} %shard_map.84.own_ref, f32[4,128,128]{2,1,0:T(8,128)S(1)} %collective-permute-done.4.other_ref), custom_call_target="tpu_custom_call" | custom-call | tf_op jit(solution)/shard_map/pallas_call | solution.py:160
  16.1 2.0 %collective-permute-done.5.refs_1_ = f32[4,32,128]{2,1,0:T(8,128)S(1)} collective-permute-done((f32[4,32,128]{2,1,0:T(8,128)S(1)}, f32[4,32,128]{2,1,0:T(8,128)S(1)}, u32[]{:S(2)}, u32[]{:S(2)}) %collective-permute-start.5) | collective-permute-done | bytes 65568 | tf_op jit(solution)/shard_map/ppermute | solution.py:220
  18.1 0.8 %shard_map.86 = f32[4,8]{1,0:T(4,128)} custom-call(f32[4,32,128]{2,1,0:T(8,128)S(1)} %shard_map.85.unit_ref, f32[4,32,128]{2,1,0:T(8,128)S(1)} %pad_maximum_fusion.refs_0_, f32[4,32,128]{2,1,0:T(8,128)S(1)} %collective-permute-done.5.refs_1_), custom_call_target="tpu_custom_call" | custom-call | tf_op jit(solution)/shard_map/pallas_call | solution.py:201
  (2 shorter events, 0.0 us)
Async XLA Ops:
  3.1 1.4 %collective-permute-start = (f32[128,128]{1,0:T(8,128)S(1)}, f32[128,128]{1,0:T(8,128)S(1)}, u32[]{:S(2)}, u32[]{:S(2)}) collective-permute-start(f32[128,128]{1,0:T(8,128)S(1)} %get-tuple-element.12.own_ref), channel_id=1, source_target_pairs={{0,1},{1,0},{2,3},{3,2},{4,5},{5,4},{6,7},{7,6},{8,9},{9,8},{10,11... | collective-permute-start | bytes 196616 | tf_op jit(solution)/shard_map/ppermute | solution.py:211
  3.6 6.6 %slice-start = ((s8[7340032]{0:T(1024)(128)(4,1)}), s8[4194304]{0:T(1024)(128)(4,1)S(1)}, s32[]{:S(2)}) async-start(s8[7340032]{0:T(1024)(128)(4,1)} %bitcast.3), calls=%async_computation | async-start | bytes 8388608
  4.4 5.8 %slice-start.1 = ((s8[7340032]{0:T(1024)(128)(4,1)}), s8[3145728]{0:T(1024)(128)(4,1)S(1)}, s32[]{:S(2)}) async-start(s8[7340032]{0:T(1024)(128)(4,1)} %bitcast.3), calls=%async_computation.1 | async-start | bytes 6291456
  4.5 5.8 %copy-start = (bf16[4,128,4096]{2,1,0:T(8,128)(2,1)S(1)}, bf16[4,128,4096]{2,1,0:T(8,128)(2,1)}, u32[]{:S(2)}) copy-start(bf16[4,128,4096]{2,1,0:T(8,128)(2,1)} %g_ref.1) | copy-start | bytes 12582916
  4.5 5.8 %copy-start.1 = (s32[4]{0:T(128)S(1)}, s32[4]{0:T(128)}, u32[]{:S(2)}) copy-start(s32[4]{0:T(128)} %lens.1) | copy-start | bytes 52
  4.9 8.3 %collective-permute-start.3 = (f32[1,32,128]{2,1,0:T(8,128)S(1)}, f32[1,32,128]{2,1,0:T(8,128)S(1)}, u32[]{:S(2)}, u32[]{:S(2)}) collective-permute-start(f32[1,32,128]{2,1,0:T(8,128)S(1)} %bitcast.5), channel_id=1, source_target_pairs={{0,13},{1,12},{2,15},{3,14},{4,9},{5,8},{6,11},{7,10},{8,5},{9,4},... | collective-permute-start | bytes 49160 | tf_op jit(solution)/shard_map/ppermute | solution.py:220
  9.6 4.1 %collective-permute-start.2 = (f32[1,32,128]{2,1,0:T(8,128)S(1)}, f32[1,32,128]{2,1,0:T(8,128)S(1)}, u32[]{:S(2)}, u32[]{:S(2)}) collective-permute-start(f32[1,32,128]{2,1,0:T(8,128)S(1)} %bitcast.6), channel_id=1, source_target_pairs={{0,9},{1,8},{2,11},{3,10},{4,13},{5,12},{6,15},{7,14},{8,1},{9,0},... | collective-permute-start | bytes 49160 | tf_op jit(solution)/shard_map/ppermute | solution.py:220
  9.6 4.1 %collective-permute-start.1 = (f32[1,32,128]{2,1,0:T(8,128)S(1)}, f32[1,32,128]{2,1,0:T(8,128)S(1)}, u32[]{:S(2)}, u32[]{:S(2)}) collective-permute-start(f32[1,32,128]{2,1,0:T(8,128)S(1)} %bitcast.7), channel_id=1, source_target_pairs={{0,5},{1,4},{2,7},{3,6},{4,1},{5,0},{6,3},{7,2},{8,13},{9,12},{10,... | collective-permute-start | bytes 49160 | tf_op jit(solution)/shard_map/ppermute | solution.py:220
  13.7 1.6 %collective-permute-start.4 = (f32[4,128,128]{2,1,0:T(8,128)S(1)}, f32[4,128,128]{2,1,0:T(8,128)S(1)}, u32[]{:S(2)}, u32[]{:S(2)}) collective-permute-start(f32[4,128,128]{2,1,0:T(8,128)S(1)} %shard_map.84.own_ref), channel_id=1, source_target_pairs={{0,1},{1,0},{2,3},{3,2},{4,5},{5,4},{6,7},{7,6},{8,9},{9,8},{10,11... | collective-permute-start | bytes 786440 | tf_op jit(solution)/shard_map/ppermute | solution.py:211
  14.0 4.1 %collective-permute-start.5 = (f32[4,32,128]{2,1,0:T(8,128)S(1)}, f32[4,32,128]{2,1,0:T(8,128)S(1)}, u32[]{:S(2)}, u32[]{:S(2)}) collective-permute-start(f32[4,32,128]{2,1,0:T(8,128)S(1)} %pad_maximum_fusion.refs_0_), channel_id=1, source_target_pairs={{0,3},{1,2},{2,1},{3,0},{4,7},{5,6},{6,5},{7,4},{8,11},{9,10},{10,... | collective-permute-start | bytes 196616 | tf_op jit(solution)/shard_map/ppermute | solution.py:220
